TPU v7x, 256 devices: a whole 4x4x8 slice. The times are simulated.
256 devices in a mesh: ctx: 32 (over x, z), cls: 8 (over y, core).
Axes of the slice: x: 4, y: 4, z: 8, core: 2. Of those that a mesh axis runs over, the one named last changes fastest.
Arguments:
- tokens: bfloat16 [196608, 8192], P(('ctx', 'cls')), may hold values from -80 to 80
- doc_length: int32 [1], replicated, may hold values from 98304 to 196608
- queries: bfloat16 [64, 8192], P('cls', 'ctx'), may hold values from -0.046875 to 0.046875
- norm_gain: float32 [8192], P('ctx'), may hold values from 0.1 to 1.9
- head_weight: bfloat16 [8192, 4096], P('ctx', 'cls'), may hold values from -0.0625 to 0.0625
- head_bias: float32 [4096], P('cls'), may hold values from -20 to 20
- labels: int32 [4096], P('cls'), may hold values 0 or 1
Outputs:
- mean_loss: float32 [], replicated
- query_grad: float32 [64, 8192], P('cls', 'ctx')
- head_grad: float32 [8192, 4096], P('ctx', 'cls')
- bias_grad: float32 [4096], P('cls')
All inputs are finite; a program needn't handle non-finite values. No bound on the sum of `labels` on one device may be relied on, other than what follows from the above.
Results may differ from a plain program's by a relative error of at most 0.017.
Values may be sent and summed in bfloat16 or wider, within the bound.
A program may use at most 64 MiB of HBM per device.

v0:
```python
import jax
import jax.numpy as jnp
from jax import lax
from jax.sharding import PartitionSpec as P


def shards(tokens, doc_length, queries, norm_gain, head_weight, head_bias, labels):
    context_count = lax.axis_size("ctx")
    class_count = lax.axis_size("cls")
    context_index = lax.axis_index("ctx")
    class_index = lax.axis_index("cls")
    token_count = tokens.shape[0]
    query_share = queries.shape[0]
    width_share = queries.shape[1]
    full_width = width_share * context_count

    def project_add(block_piece):
        return lax.dot_general(
            block_piece, tokens, (((1,), (1,)), ((), ())), preferred_element_type=jnp.float32
        )

    query_block = lax.all_gather(queries, "cls", axis=0, tiled=True)
    scores = project_add(lax.all_gather(query_block, "ctx", axis=1, tiled=True))
    offset = (context_index * class_count + class_index) * token_count
    position = offset + jnp.arange(token_count, dtype=jnp.int32)
    valid_mask = (position < doc_length[0])[None, :]
    local_peak = jnp.max(jnp.where(valid_mask, scores, -1e30), axis=1)
    peak = lax.pmax(local_peak, ("ctx", "cls"))
    weights = jnp.exp(jnp.where(valid_mask, scores - peak[:, None], -1e30))
    pooled_part = jnp.dot(weights.astype(jnp.bfloat16), tokens, preferred_element_type=jnp.float32)
    whole_sum = lax.psum(pooled_part, ("ctx", "cls"))
    pooled = lax.dynamic_slice(
        whole_sum,
        (class_index * query_share, context_index * width_share),
        (query_share, width_share),
    )
    scaled_b = (pooled * norm_gain[None, :]).astype(jnp.bfloat16)
    head_blocks = head_weight.reshape(width_share, query_share, -1)
    square_part = jnp.sum(pooled * pooled, axis=1)
    logit_part = jnp.einsum("hd,dha->ha", scaled_b, head_blocks, preferred_element_type=jnp.float32)
    squares, logit_raw = lax.psum((square_part, logit_part), "ctx")
    inverse_rms = lax.rsqrt(squares / full_width + 1e-05)
    logits = inverse_rms[:, None] * logit_raw + head_bias.reshape(query_share, -1)
    target = labels.reshape(query_share, -1).astype(jnp.float32)
    loss_part = jnp.sum(jax.nn.softplus(logits) - target * logits)
    mean_loss = lax.psum(loss_part, "cls") / (labels.shape[0] * class_count)
    logit_grad = jax.nn.sigmoid(logits) - target
    normed = pooled * inverse_rms[:, None] * norm_gain[None, :]
    head_grad = jnp.einsum("hd,ha->dha", normed, logit_grad).reshape(width_share, -1)
    normed_grad = (
        jnp.einsum("dha,ha->hd", head_blocks.astype(jnp.float32), logit_grad) * norm_gain[None, :]
    )
    unit_pooled = pooled * inverse_rms[:, None]
    inner_part = jnp.sum(unit_pooled * normed_grad, axis=1)
    inner_mean = lax.psum(inner_part, "ctx") / full_width
    pooled_grad = (inverse_rms[:, None] * (normed_grad - unit_pooled * inner_mean[:, None])).astype(
        jnp.bfloat16
    )
    grad_block = lax.all_gather(pooled_grad, "cls", axis=0, tiled=True)
    projected = project_add(lax.all_gather(grad_block, "ctx", axis=1, tiled=True))
    score_grad = (weights * projected).astype(jnp.bfloat16)
    query_part = jnp.dot(score_grad, tokens, preferred_element_type=jnp.float32)
    column_grad = lax.psum_scatter(query_part, "ctx", scatter_dimension=1, tiled=True)
    query_grad = lax.psum_scatter(column_grad, "cls", scatter_dimension=0, tiled=True)
    return (mean_loss, query_grad, head_grad, logit_grad.reshape(-1))


def solution(mesh):
    return jax.shard_map(
        shards,
        mesh=mesh,
        in_specs=(
            P(("ctx", "cls"), None),
            P(),
            P("cls", "ctx"),
            P("ctx"),
            P("ctx", "cls"),
            P("cls"),
            P("cls"),
        ),
        out_specs=(P(), P("cls", "ctx"), P("ctx", "cls"), P("cls")),
        check_vma=False,
    )
```

profile of v0, /device:TPU:2, one launch (start us, length us, event | category | flops | bytes accessed | tf_op | source)
XLA Modules:
  0.0 943.6 jit_solution(2797138843445842792)
XLA Ops:
  7.2 14.3 %all_gather.12 = bf16[64,256]{1,0:T(8,128)(2,1)} all-gather(bf16[8,256]{1,0:T(8,128)(2,1)} %param.9), channel_id=1, replica_groups=mesh['ctx'=32,'cls'=8] {'cls'}, dimensions={0}, use_global_device_ids=true | all-gather | bytes 36864 | tf_op jit(solution)/shard_map/all_gather | solution.py:22
  22.3 72.8 %all-gather.3.cloned.1.call-done = bf16[64,8192]{1,0:T(8,128)(2,1)} async-done(((bf16[64,256]{1,0:T(8,128)(2,1)}), bf16[64,8192]{1,0:T(8,128)(2,1)}) %all-gather.3.cloned.1.call-update) | async-done | bytes 1048592 | tf_op jit(solution)/shard_map/all_gather | solution.py:23
  95.0 8.9 select_reduce_fusion
  104.0 74.6 %pmax.7 = f32[64]{0:T(128)S(1)} all-reduce(f32[64]{0:T(128)S(1)} %get-tuple-element.16), channel_id=1, replica_groups=mesh['ctx'=32,'cls'=8] {'ctx','cls'}, use_global_device_ids=true, to_apply=%region_1.2 | all-reduce | flops 64 | bytes 512 | tf_op jit(solution)/shard_map/pmax | solution.py:28
  178.6 8.2 fusion.3
  187.0 0.1 copy.12
  187.3 257.2 %all-reduce.3.cloned.1.call-done = f32[64,8192]{1,0:T(8,128)} async-done(((f32[64,8192]{1,0:T(8,128)}), f32[64,8192]{1,0:T(8,128)}) %all-reduce.3.cloned.1.call-update) | async-done | bytes 2097168 | tf_op jit(solution)/shard_map/psum | solution.py:31
  444.5 0.8 multiply_reduce_fusion.1
  445.3 0.2 fusion.11
  445.5 61.5 %all-reduce = (f32[8,64]{1,0:T(8,128)S(1)}, f32[8]{0:T(128)S(1)}) all-reduce(f32[8,64]{1,0:T(8,128)S(1)} %bitcast.32, f32[8]{0:T(128)S(1)} %get-tuple-element.12), channel_id=1, replica_groups=mesh['ctx'=32,'cls'=8] {'ctx'}, use_global_device_ids=true, to_apply=%region_5.6 | all-reduce | flops 520 | bytes 4160 | tf_op jit(solution)/shard_map/psum | solution.py:41
  507.0 0.7 divide_subtract_fusion
  507.7 0.1 fusion.18
  507.8 0.9 multiply_multiply_fusion
  508.7 69.2 %psum.39 = f32[8]{0:T(128)S(1)} all-reduce(f32[8]{0:T(128)S(1)} %get-tuple-element.11), channel_id=1, replica_groups=mesh['ctx'=32,'cls'=8] {'ctx'}, use_global_device_ids=true, to_apply=%region_9.10 | all-reduce | flops 8 | bytes 64 | tf_op jit(solution)/shard_map/psum | solution.py:55
  577.9 0.8 multiply_convert_fusion
  578.7 13.7 %all_gather.14 = bf16[64,256]{1,0:T(8,128)(2,1)} all-gather(bf16[8,256]{1,0:T(8,128)(2,1)S(1)} %multiply_convert_fusion), channel_id=1, replica_groups=mesh['ctx'=32,'cls'=8] {'cls'}, dimensions={0}, use_global_device_ids=true | all-gather | bytes 36864 | tf_op jit(solution)/shard_map/all_gather | solution.py:59
  592.4 0.2 reduce-scatter.3.cloned.1.call-start
  592.6 76.7 %all-gather.5.cloned.1.call-done = bf16[64,8192]{1,0:T(8,128)(2,1)} async-done(((bf16[64,256]{1,0:T(8,128)(2,1)}), bf16[64,8192]{1,0:T(8,128)(2,1)}) %all-gather.5.cloned.1.call-update) | async-done | bytes 1048592 | tf_op jit(solution)/shard_map/all_gather | solution.py:60
  669.4 17.7 %fusion.1 = f32[64,8192]{1,0:T(8,128)} fusion(bf16[768,8192]{1,0:T(8,128)(2,1)} %param.7, bf16[64,8192]{1,0:T(8,128)(2,1)} %all-gather.5.cloned.1.call-done, f32[64,768]{1,0:T(8,128)S(1)} %get-tuple-element.17, f32[64]{0:T(128)S(1)} %pmax.7, pred[768]{0:T(1024)(128)(4,1)S(1)} %add_compare_fusion), kind=kOutput, calls=%fused_computation.2 | convolution fusion | flops 1610809344 | bytes 15926272 | tf_op jit(solution)/shard_map/dot_general | solution.py:62
  687.2 13.1 %psum.38 = f32[]{:T(128)} all-reduce(f32[]{:T(128)} %get-tuple-element.15), channel_id=1, replica_groups=mesh['ctx'=32,'cls'=8] {'cls'}, use_global_device_ids=true, to_apply=%region_7.8 | all-reduce | flops 1 | bytes 8 | tf_op jit(solution)/shard_map/psum | solution.py:46
  700.2 0.7 reshape.34
  700.9 200.1 %reduce-scatter.3.cloned.1.call-done = f32[64,256]{1,0:T(8,128)} async-done(((f32[64,8192]{1,0:T(8,128)}), f32[64,256]{1,0:T(8,128)}) %reduce-scatter.3.cloned.1.call-update) | async-done | bytes 65552 | tf_op jit(solution)/shard_map/reduce_scatter | solution.py:63
  901.1 1.0 copy.13
  902.8 33.2 %reduce-scatter.5.cloned.1.call-done = f32[8,256]{1,0:T(8,128)} async-done(((f32[64,256]{1,0:T(8,128)}), f32[8,256]{1,0:T(8,128)}) %reduce-scatter.5.cloned.1.call-update) | async-done | bytes 8208 | tf_op jit(solution)/shard_map/reduce_scatter | solution.py:64
  (24 shorter events, 0.6 us)
Async XLA Ops:
  7.2 87.9 %all-gather.3.cloned.1.call-start = ((), (), s32[]{:S(2)}) async-start(), calls=%async_computation.2 | async-start | bytes 1081344 | tf_op jit(solution)/shard_map/all_gather | solution.py:23
  21.6 422.9 %all-reduce.3.cloned.1.call-start = ((), (), s32[]{:S(2)}) async-start(), calls=%async_computation.3 | async-start | bytes 4194304 | tf_op jit(solution)/shard_map/psum | solution.py:31
  104.0 83.0 %copy-start = (bf16[256,512]{1,0:T(8,128)(2,1)S(1)}, bf16[256,512]{1,0:T(8,128)(2,1)}, u32[]{:S(2)}) copy-start(bf16[256,512]{1,0:T(8,128)(2,1)} %param.11) | copy-start | bytes 786436
  104.0 83.1 %copy-start.3 = (s32[512]{0:T(512)S(1)}, s32[512]{0:T(512)}, u32[]{:S(2)}) copy-start(s32[512]{0:T(512)} %param.13) | copy-start | bytes 6148
  104.0 83.2 %copy-start.2 = (f32[512]{0:T(512)S(1)}, f32[512]{0:T(512)}, u32[]{:S(2)}) copy-start(f32[512]{0:T(512)} %param.12) | copy-start | bytes 6148
  104.0 340.5 %copy-start.1 = (f32[256]{0:T(256)S(1)}, f32[256]{0:T(256)}, u32[]{:S(2)}) copy-start(f32[256]{0:T(256)} %param.10) | copy-start | bytes 3076
  186.9 482.5 %all-gather.5.cloned.1.call-start = ((), (), s32[]{:S(2)}) async-start(), calls=%async_computation.4 | async-start | bytes 1081344 | tf_op jit(solution)/shard_map/all_gather | solution.py:60
  592.4 308.6 %reduce-scatter.3.cloned.1.call-start = ((), (), s32[]{:S(2)}) async-start(), calls=%async_computation.5 | async-start | bytes 2162688 | tf_op jit(solution)/shard_map/reduce_scatter | solution.py:63
  687.1 248.9 %reduce-scatter.5.cloned.1.call-start = ((), (), s32[]{:S(2)}) async-start(), calls=%async_computation.6 | async-start | bytes 73728 | tf_op jit(solution)/shard_map/reduce_scatter | solution.py:64
Sparse Core Ops, SparseCore 0:
  21.7 73.3 all-gather.2
  187.0 257.4 all-reduce.2
  592.5 76.7 all-gather.4
  687.2 213.7 reduce-scatter.2
  904.0 31.8 reduce-scatter.4
where the time goes:
time: 944 us
  waiting for transfers between devices  640 us (68%)
  blocking collectives  246 us (26%)
  matrix products  35.2 us (4%)
  between operations  16.3 us (2%)
    psum x1, waiting for transfers between devices, shards(): whole_sum = lax.psum(pooled_part, ('ctx', 'cls'))  257 us
    reduce_scatter x1, waiting for transfers between devices, shards(): lax.psum_scatter(query_part, 'ctx', scatter_dimension=1, tiled=True)  200 us
    all_gather x1, waiting for transfers between devices, shards(): lax.all_gather(grad_block, 'ctx', axis=1, tiled=True)  76.7 us
    pmax x1, blocking collectives, shards(): peak = lax.pmax(local_peak, ('ctx', 'cls'))  74.6 us
    all_gather x1, waiting for transfers between devices, shards(): scores = project_add(lax.all_gather(query_block, 'ctx', axis=1, tiled=True))  72.8 us
    psum x1, blocking collectives, shards(): inner_mean = lax.psum(inner_part, 'ctx') / full_width  69.2 us
    psum x1, blocking collectives, shards(): squares, logit_raw = lax.psum((square_part, logit_part), 'ctx')  61.5 us
    reduce_scatter x1, waiting for transfers between devices, shards(): lax.psum_scatter(column_grad, 'cls', scatter_dimension=0, tiled=True)  33.2 us
  transfers between devices with their start and end apart: 5, of which 5 were waited for; matrix products, arithmetic and copies ran while one was open for 0% of the time, Pallas kernels for 0%

commit v1 on v0

--- a/solution.py
+++ b/solution.py
@@ -28,7 +28,7 @@
     peak = lax.pmax(local_peak, ("ctx", "cls"))
     weights = jnp.exp(jnp.where(valid_mask, scores - peak[:, None], -1e30))
     pooled_part = jnp.dot(weights.astype(jnp.bfloat16), tokens, preferred_element_type=jnp.float32)
-    whole_sum = lax.psum(pooled_part, ("ctx", "cls"))
+    whole_sum = lax.psum(lax.psum(pooled_part, "ctx"), "cls")
     pooled = lax.dynamic_slice(
         whole_sum,
         (class_index * query_share, context_index * width_share),

time: 944 us -> 911 us (0.965)
  waiting for transfers between devices: 640 us -> 603 us
    psum x1 -> x2, waiting for transfers between devices: 257 us -> 220 us  [shards(): whole_sum = lax.psum(lax.psum(pooled_part, 'ctx'), 'cls')]
  transfers between devices with their start and end apart: 5 -> 6, of which waited for: 5 -> 6; matrix products, arithmetic and copies ran while one was open for 0% -> 0% of each run, Pallas kernels for 0% -> 0%
where the time goes in v1:
time: 911 us; the launch traced here: 910 us
  waiting for transfers between devices  603 us (66%)
  blocking collectives  249 us (27%)
  matrix products  35.2 us (4%)
  between operations  16.7 us (2%)
    psum x2, waiting for transfers between devices, shards(): whole_sum = lax.psum(lax.psum(pooled_part, 'ctx'), 'cls')  220 us
    reduce_scatter x1, waiting for transfers between devices, shards(): lax.psum_scatter(query_part, 'ctx', scatter_dimension=1, tiled=True)  200 us
    all_gather x1, waiting for transfers between devices, shards(): lax.all_gather(grad_block, 'ctx', axis=1, tiled=True)  76.6 us
    pmax x1, blocking collectives, shards(): peak = lax.pmax(local_peak, ('ctx', 'cls'))  74.6 us
    all_gather x1, waiting for transfers between devices, shards(): scores = project_add(lax.all_gather(query_block, 'ctx', axis=1, tiled=True))  72.8 us
    psum x1, blocking collectives, shards(): inner_mean = lax.psum(inner_part, 'ctx') / full_width  69.3 us
    psum x1, blocking collectives, shards(): squares, logit_raw = lax.psum((square_part, logit_part), 'ctx')  64.3 us
    reduce_scatter x1, waiting for transfers between devices, shards(): lax.psum_scatter(column_grad, 'cls', scatter_dimension=0, tiled=True)  33.1 us
  transfers between devices with their start and end apart: 6, of which 6 were waited for; matrix products, arithmetic and copies ran while one was open for 0% of the time, Pallas kernels for 0%

profile of v1, /device:TPU:2, one launch (start us, length us, event | category | flops | bytes accessed | tf_op | source)
XLA Modules:
  0.0 910.0 jit_solution(14745303493818176154)
XLA Ops:
  7.2 14.3 %all_gather.12 = bf16[64,256]{1,0:T(8,128)(2,1)} all-gather(bf16[8,256]{1,0:T(8,128)(2,1)} %param.9), channel_id=1, replica_groups=mesh['ctx'=32,'cls'=8] {'cls'}, dimensions={0}, use_global_device_ids=true | all-gather | bytes 36864 | tf_op jit(solution)/shard_map/all_gather | solution.py:22
  22.3 72.8 %all-gather.3.cloned.1.call-done = bf16[64,8192]{1,0:T(8,128)(2,1)} async-done(((bf16[64,256]{1,0:T(8,128)(2,1)}), bf16[64,8192]{1,0:T(8,128)(2,1)}) %all-gather.3.cloned.1.call-update) | async-done | bytes 1048592 | tf_op jit(solution)/shard_map/all_gather | solution.py:23
  95.0 8.9 select_reduce_fusion
  104.0 74.6 %pmax.7 = f32[64]{0:T(128)S(1)} all-reduce(f32[64]{0:T(128)S(1)} %get-tuple-element.16), channel_id=1, replica_groups=mesh['ctx'=32,'cls'=8] {'ctx','cls'}, use_global_device_ids=true, to_apply=%region_1.2 | all-reduce | flops 64 | bytes 512 | tf_op jit(solution)/shard_map/pmax | solution.py:28
  178.7 8.2 fusion.3
  187.0 149.0 %all-reduce.4.cloned.1.call-done = f32[64,8192]{1,0:T(8,128)} async-done(((f32[64,8192]{1,0:T(8,128)}), f32[64,8192]{1,0:T(8,128)}) %all-reduce.4.cloned.1.call-update) | async-done | bytes 2097168 | tf_op jit(solution)/shard_map/psum | solution.py:31
  336.4 71.5 %all-reduce.6.cloned.1.call-done = f32[64,8192]{1,0:T(8,128)} async-done(((f32[64,8192]{1,0:T(8,128)}), f32[64,8192]{1,0:T(8,128)}) %all-reduce.6.cloned.1.call-update) | async-done | bytes 2097168 | tf_op jit(solution)/shard_map/psum | solution.py:31
  407.9 0.8 multiply_reduce_fusion.1
  408.7 0.2 fusion.11
  408.8 64.3 %all-reduce = (f32[8,64]{1,0:T(8,128)S(1)}, f32[8]{0:T(128)S(1)}) all-reduce(f32[8,64]{1,0:T(8,128)S(1)} %bitcast.32, f32[8]{0:T(128)S(1)} %get-tuple-element.12), channel_id=1, replica_groups=mesh['ctx'=32,'cls'=8] {'ctx'}, use_global_device_ids=true, to_apply=%region_6.7 | all-reduce | flops 520 | bytes 4160 | tf_op jit(solution)/shard_map/psum | solution.py:41
  473.2 0.7 divide_subtract_fusion
  473.9 0.1 fusion.18
  474.0 0.9 multiply_multiply_fusion
  474.9 69.3 %psum.47 = f32[8]{0:T(128)S(1)} all-reduce(f32[8]{0:T(128)S(1)} %get-tuple-element.11), channel_id=1, replica_groups=mesh['ctx'=32,'cls'=8] {'ctx'}, use_global_device_ids=true, to_apply=%region_10.11 | all-reduce | flops 8 | bytes 64 | tf_op jit(solution)/shard_map/psum | solution.py:55
  544.2 0.8 multiply_convert_fusion
  545.0 13.7 %all_gather.14 = bf16[64,256]{1,0:T(8,128)(2,1)} all-gather(bf16[8,256]{1,0:T(8,128)(2,1)S(1)} %multiply_convert_fusion), channel_id=1, replica_groups=mesh['ctx'=32,'cls'=8] {'cls'}, dimensions={0}, use_global_device_ids=true | all-gather | bytes 36864 | tf_op jit(solution)/shard_map/all_gather | solution.py:59
  558.7 0.2 reduce-scatter.3.cloned.1.call-start
  558.9 76.6 %all-gather.5.cloned.1.call-done = bf16[64,8192]{1,0:T(8,128)(2,1)} async-done(((bf16[64,256]{1,0:T(8,128)(2,1)}), bf16[64,8192]{1,0:T(8,128)(2,1)}) %all-gather.5.cloned.1.call-update) | async-done | bytes 1048592 | tf_op jit(solution)/shard_map/all_gather | solution.py:60
  635.5 17.7 %fusion.1 = f32[64,8192]{1,0:T(8,128)} fusion(bf16[768,8192]{1,0:T(8,128)(2,1)} %param.7, bf16[64,8192]{1,0:T(8,128)(2,1)} %all-gather.5.cloned.1.call-done, f32[64,768]{1,0:T(8,128)S(1)} %get-tuple-element.17, f32[64]{0:T(128)S(1)} %pmax.7, pred[768]{0:T(1024)(128)(4,1)S(1)} %add_compare_fusion), kind=kOutput, calls=%fused_computation.2 | convolution fusion | flops 1610809344 | bytes 15926272 | tf_op jit(solution)/shard_map/dot_general | solution.py:62
  653.3 13.1 %psum.46 = f32[]{:T(128)} all-reduce(f32[]{:T(128)} %get-tuple-element.15), channel_id=1, replica_groups=mesh['ctx'=32,'cls'=8] {'cls'}, use_global_device_ids=true, to_apply=%region_8.9 | all-reduce | flops 1 | bytes 8 | tf_op jit(solution)/shard_map/psum | solution.py:46
  666.4 0.7 reshape.34
  667.0 200.1 %reduce-scatter.3.cloned.1.call-done = f32[64,256]{1,0:T(8,128)} async-done(((f32[64,8192]{1,0:T(8,128)}), f32[64,256]{1,0:T(8,128)}) %reduce-scatter.3.cloned.1.call-update) | async-done | bytes 65552 | tf_op jit(solution)/shard_map/reduce_scatter | solution.py:63
  867.3 1.0 copy.13
  869.0 33.1 %reduce-scatter.5.cloned.1.call-done = f32[8,256]{1,0:T(8,128)} async-done(((f32[64,256]{1,0:T(8,128)}), f32[8,256]{1,0:T(8,128)}) %reduce-scatter.5.cloned.1.call-update) | async-done | bytes 8208 | tf_op jit(solution)/shard_map/reduce_scatter | solution.py:64
  (27 shorter events, 0.8 us)
Async XLA Ops:
  7.2 87.9 %all-gather.3.cloned.1.call-start = ((), (), s32[]{:S(2)}) async-start(), calls=%async_computation.2 | async-start | bytes 1081344 | tf_op jit(solution)/shard_map/all_gather | solution.py:23
  21.6 314.4 %all-reduce.4.cloned.1.call-start = ((), (), s32[]{:S(2)}) async-start(), calls=%async_computation.3 | async-start | bytes 4194304 | tf_op jit(solution)/shard_map/psum | solution.py:31
  104.0 232.0 %copy-start = (bf16[256,512]{1,0:T(8,128)(2,1)S(1)}, bf16[256,512]{1,0:T(8,128)(2,1)}, u32[]{:S(2)}) copy-start(bf16[256,512]{1,0:T(8,128)(2,1)} %param.11) | copy-start | bytes 786436
  104.0 232.2 %copy-start.3 = (s32[512]{0:T(512)S(1)}, s32[512]{0:T(512)}, u32[]{:S(2)}) copy-start(s32[512]{0:T(512)} %param.13) | copy-start | bytes 6148
  104.0 232.3 %copy-start.2 = (f32[512]{0:T(512)S(1)}, f32[512]{0:T(512)}, u32[]{:S(2)}) copy-start(f32[512]{0:T(512)} %param.12) | copy-start | bytes 6148
  104.0 303.8 %copy-start.1 = (f32[256]{0:T(256)S(1)}, f32[256]{0:T(256)}, u32[]{:S(2)}) copy-start(f32[256]{0:T(256)} %param.10) | copy-start | bytes 3076
  186.9 220.9 %all-reduce.6.cloned.1.call-start = ((), (), s32[]{:S(2)}) async-start(), calls=%async_computation.4 | async-start | bytes 4194304 | tf_op jit(solution)/shard_map/psum | solution.py:31
  336.0 299.5 %all-gather.5.cloned.1.call-start = ((), (), s32[]{:S(2)}) async-start(), calls=%async_computation.5 | async-start | bytes 1081344 | tf_op jit(solution)/shard_map/all_gather | solution.py:60
  558.7 308.5 %reduce-scatter.3.cloned.1.call-start = ((), (), s32[]{:S(2)}) async-start(), calls=%async_computation.6 | async-start | bytes 2162688 | tf_op jit(solution)/shard_map/reduce_scatter | solution.py:63
  653.3 248.8 %reduce-scatter.5.cloned.1.call-start = ((), (), s32[]{:S(2)}) async-start(), calls=%async_computation.7 | async-start | bytes 73728 | tf_op jit(solution)/shard_map/reduce_scatter | solution.py:64
Sparse Core Ops, SparseCore 0:
  21.7 73.3 all-gather.2
  187.0 148.8 all-reduce.3
  338.5 69.3 all-reduce.5
  558.8 76.6 all-gather.4
  653.4 213.7 reduce-scatter.2
  870.1 31.9 reduce-scatter.4
